TPU v7x, 32 devices: a whole 2x2x4 slice. The times are simulated.
32 devices in a mesh: fsdp: 8 (over z, core), batch: 4 (over y, x).
Axes of the slice: x: 2, y: 2, z: 4, core: 2. Of those that a mesh axis runs over, the one named last changes fastest.
Arguments:
- latents: bfloat16 [4, 8, 1024, 640], P('batch', 'fsdp'), may hold values from -6 to 6
- norm_gain: float32 [640], replicated, may hold values from 0.25 to 1.75
- second_gain: float32 [640], replicated, may hold values from 0.25 to 1.75
- spatial_w: bfloat16 [9, 640, 640], P(None, None, 'fsdp'), may hold values from -0.078125 to 0.078125
- temporal_w: bfloat16 [3, 640, 640], P(None, None, 'fsdp'), may hold values from -0.125 to 0.125
- critic_w: bfloat16 [4, 640, 640], P('batch'), may hold values from -0.25 to 0.25
- critic_head: float32 [4, 640], P('batch'), may hold values from -6 to 6
- targets: int32 [4, 32, 1], P('batch'), may hold values from 0 to 3; in each aligned block of 32 rows (0 to 31, 32 to 63, ..., all dimensions but the last counted through in order) at most 16 rows name the same one
- feasible: int32 [4, 8], P('batch', 'fsdp'), may hold values 0 or 1
Outputs:
- guided: bfloat16 [4, 8, 1024, 640], P('batch', 'fsdp')
Inputs may be any that keep to these rules, and one draw needn't show every extreme that they name: `targets`: among one candidate's 32 rows no critic group is named more than 16 times.
All inputs are finite; a program needn't handle non-finite values. No bound on the sum of `feasible` on one device may be relied on, other than what follows from the above.
Results may differ from a plain program's by a relative error of at most 0.0065.
Values may be sent and summed in bfloat16 or wider, within the bound.
A program may use at most 128 MiB of HBM per device.

v0:
```python
import jax
import jax.numpy as jnp
from jax import lax
from jax.sharding import PartitionSpec as P

GROUPS = 32
IMG_ROWS = 32
IMG_COLS = 32
PIX = 1024


def with_halo(array, sides, width):
    for axis, dim in sides:
        size, length = (lax.axis_size(axis), array.shape[dim])
        up = [(i, (i + 1) % size) for i in range(size - 1)]
        down = [(j, i) for i, j in up]
        last = lax.slice_in_dim(array, length - width, length, axis=dim)
        leading = lax.slice_in_dim(array, 0, width, axis=dim)
        before = lax.ppermute(last, axis, up)
        after = lax.ppermute(leading, axis, down)
        array = jnp.concatenate([before, array, after], axis=dim)
    return array


def group_silu(values, gain):
    shape = values.shape
    width = shape[-1]
    grouped = values.astype(jnp.float32).reshape(-1, shape[-2], GROUPS, width // GROUPS)
    center = jnp.mean(grouped, axis=(1, 3), keepdims=True)
    spread = jnp.mean((grouped - center) ** 2, axis=(1, 3), keepdims=True)
    normed = ((grouped - center) * lax.rsqrt(spread + 1e-05)).reshape(shape) * gain
    return jax.nn.silu(normed).astype(jnp.bfloat16)


def per_device(
    latents, norm_gain, second_gain, spatial_w, temporal_w, critic_w, critic_head, targets, feasible
):
    cands = latents.shape[0]
    width = latents.shape[-1]
    first = group_silu(latents, norm_gain)
    padded = jnp.pad(
        first.reshape(cands, IMG_ROWS, IMG_COLS, width), ((0, 0), (1, 1), (1, 1), (0, 0))
    )
    piece = lax.all_gather(spatial_w, "fsdp", axis=2, tiled=True)
    total = jnp.zeros((cands * PIX, piece.shape[2]), jnp.float32)
    for offset in range(9):
        row_off, col_off = divmod(offset, 3)
        window = padded[:, row_off : row_off + IMG_ROWS, col_off : col_off + IMG_COLS].reshape(
            -1, width
        )
        total = total + jnp.dot(window, piece[offset], preferred_element_type=jnp.float32)
    mixed = total
    section = (latents.astype(jnp.float32) + mixed.reshape(latents.shape)).astype(jnp.bfloat16)
    second = group_silu(section, second_gain)
    beside_all = with_halo(second, (("fsdp", 1),), 1)
    piece = lax.all_gather(temporal_w, "fsdp", axis=2, tiled=True)
    total = jnp.zeros((cands * PIX, piece.shape[2]), jnp.float32)
    for tap in range(3):
        total = total + jnp.dot(
            beside_all[:, tap].reshape(-1, width), piece[tap], preferred_element_type=jnp.float32
        )
    denoised = (section.astype(jnp.float32) + total.reshape(latents.shape)).astype(jnp.bfloat16)
    groups = lax.axis_size("batch")
    capacity = max(2, 2 * IMG_ROWS // groups)
    slots = cands * capacity
    flat_targets = targets.reshape(-1)
    chosen = (flat_targets[:, None] == jnp.arange(groups, dtype=jnp.int32)[None, :]).astype(
        jnp.int32
    )
    earlier = jnp.cumsum(chosen, axis=0) - chosen
    slot_of = jnp.sum(earlier * chosen, axis=1)
    live = jnp.repeat(feasible.reshape(-1), IMG_ROWS) > 0
    position = flat_targets * slots + slot_of
    placing = (
        (jnp.arange(groups * slots, dtype=jnp.int32)[:, None] == position[None, :]) & live[None, :]
    ).astype(jnp.bfloat16)
    rows = denoised.reshape(cands * IMG_ROWS, IMG_COLS * width)
    outgoing = (
        jnp.dot(placing, rows, preferred_element_type=jnp.float32)
        .astype(jnp.bfloat16)
        .reshape(groups, slots, IMG_COLS * width)
    )
    weights = lax.all_gather(critic_w, "batch", axis=0, tiled=True)
    heads = lax.all_gather(critic_head.astype(jnp.bfloat16), "batch", axis=0, tiled=True).astype(
        jnp.float32
    )
    count = weights.shape[0]
    block = outgoing.reshape(count, -1, width)
    pre = jnp.einsum("gtc,gch->gth", block, weights, preferred_element_type=jnp.float32)
    slope = ((1.0 - jnp.tanh(pre) ** 2) * heads[:, None, :]).astype(jnp.bfloat16)
    grads = jnp.einsum("gth,gch->gtc", slope, weights, preferred_element_type=jnp.float32).astype(
        jnp.bfloat16
    )
    returned = grads.reshape(count, slots, -1)
    back = jnp.dot(
        placing.T, returned.reshape(groups * slots, -1), preferred_element_type=jnp.float32
    )
    guided = (rows.astype(jnp.float32) - back).astype(jnp.bfloat16)
    return guided.reshape(latents.shape)


def solution(mesh):
    in_specs = (
        P("batch", "fsdp", None, None),
        P(),
        P(),
        P(None, None, "fsdp"),
        P(None, None, "fsdp"),
        P("batch", None, None),
        P("batch", None),
        P("batch", None, None),
        P("batch", "fsdp"),
    )
    out_specs = P("batch", "fsdp", None, None)
    return jax.shard_map(
        per_device, mesh=mesh, in_specs=in_specs, out_specs=out_specs, check_vma=False
    )
```

profile of v0, /device:TPU:0, one launch (start us, length us, event | category | flops | bytes accessed | tf_op | source)
XLA Modules:
  0.0 190.4 jit_solution(17490890075055864278)
XLA Ops:
  6.5 0.7 all-gather.5.cloned.1.call-update
  7.3 0.7 all-gather.7.cloned.1.call-update
  8.1 0.7 all-gather.9.cloned.1.call-update
  9.4 0.4 fusion.13
  10.2 0.8 fusion.20
  11.1 5.3 %pad_slice_fusion = (bf16[1,32,32,640]{3,2,1,0:T(8,128)(2,1)}, bf16[1,32,32,640]{3,2,1,0:T(8,128)(2,1)}, bf16[1,32,32,640]{3,2,1,0:T(8,128)(2,1)}, bf16[1,32,32,...) fusion(bf16[1,32,32,640]{3,2,1,0:T(8,128)(2,1)S(1)} %bitcast.88), kind=kLoop, calls=%fused_computation.36 | loop fusion | bytes 11796480 | tf_op jit(solution)/shard_map/slice | solution.py:48
  16.4 69.0 %all-gather.5.cloned.1.call-done = bf16[9,640,640]{1,2,0:T(8,128)(2,1)} async-done(((bf16[9,640,80]{1,2,0:T(8,128)(2,1)}), bf16[9,640,640]{1,2,0:T(8,128)(2,1)}) %all-gather.5.cloned.1.call-update) | async-done | bytes 7372816 | tf_op jit(solution)/shard_map/all_gather | solution.py:44
  85.4 2.6 %fusion.35 = f32[1024,640]{1,0:T(8,128)S(1)} fusion(bf16[1,1,1024,640]{3,2,1,0:T(8,128)(2,1)S(1)} %fusion.20, bf16[9,640,640]{1,2,0:T(8,128)(2,1)} %all-gather.5.cloned.1.call-done), kind=kOutput, calls=%fused_computation.50 | convolution fusion | flops 838860800 | bytes 4751360 | tf_op jit(solution)/shard_map/dot_general | solution.py:51
  88.0 2.6 %fusion.39 = f32[1024,640]{1,0:T(8,128)S(1)} fusion(bf16[1024,640]{1,0:T(8,128)(2,1)S(1)} %bitcast.96, bf16[9,640,640]{1,2,0:T(8,128)(2,1)} %all-gather.5.cloned.1.call-done), kind=kOutput, calls=%fused_computation.58 | convolution fusion | flops 838860800 | bytes 4751360 | tf_op jit(solution)/shard_map/dot_general | solution.py:51
  90.6 2.6 %fusion.40 = f32[1024,640]{1,0:T(8,128)S(1)} fusion(bf16[1024,640]{1,0:T(8,128)(2,1)S(1)} %bitcast.95, bf16[9,640,640]{1,2,0:T(8,128)(2,1)} %all-gather.5.cloned.1.call-done), kind=kOutput, calls=%fused_computation.60 | convolution fusion | flops 838860800 | bytes 4751360 | tf_op jit(solution)/shard_map/dot_general | solution.py:51
  93.2 2.7 %fusion.41 = f32[1024,640]{1,0:T(8,128)S(1)} fusion(bf16[1024,640]{1,0:T(8,128)(2,1)S(1)} %bitcast.94, bf16[9,640,640]{1,2,0:T(8,128)(2,1)} %all-gather.5.cloned.1.call-done), kind=kOutput, calls=%fused_computation.62 | convolution fusion | flops 838860800 | bytes 4751360 | tf_op jit(solution)/shard_map/dot_general | solution.py:51
  95.9 2.6 %fusion.42 = f32[1024,640]{1,0:T(8,128)S(1)} fusion(bf16[1024,640]{1,0:T(8,128)(2,1)S(1)} %bitcast.93, bf16[9,640,640]{1,2,0:T(8,128)(2,1)} %all-gather.5.cloned.1.call-done), kind=kOutput, calls=%fused_computation.65 | convolution fusion | flops 838860800 | bytes 4751360 | tf_op jit(solution)/shard_map/dot_general | solution.py:51
  98.5 2.6 %fusion.43 = f32[1024,640]{1,0:T(8,128)S(1)} fusion(bf16[1024,640]{1,0:T(8,128)(2,1)S(1)} %bitcast.92, bf16[9,640,640]{1,2,0:T(8,128)(2,1)} %all-gather.5.cloned.1.call-done), kind=kOutput, calls=%fused_computation.67 | convolution fusion | flops 838860800 | bytes 4751360 | tf_op jit(solution)/shard_map/dot_general | solution.py:51
  101.1 2.6 %fusion.44 = f32[1024,640]{1,0:T(8,128)S(1)} fusion(bf16[1024,640]{1,0:T(8,128)(2,1)S(1)} %bitcast.91, bf16[9,640,640]{1,2,0:T(8,128)(2,1)} %all-gather.5.cloned.1.call-done), kind=kOutput, calls=%fused_computation.69 | convolution fusion | flops 838860800 | bytes 4751360 | tf_op jit(solution)/shard_map/dot_general | solution.py:51
  103.7 4.1 %fusion.45 = f32[1024,640]{1,0:T(8,128)} fusion(bf16[1024,640]{1,0:T(8,128)(2,1)S(1)} %bitcast.90, bf16[9,640,640]{1,2,0:T(8,128)(2,1)} %all-gather.5.cloned.1.call-done), kind=kOutput, calls=%fused_computation.71 | convolution fusion | flops 838860800 | bytes 4751360 | tf_op jit(solution)/shard_map/dot_general | solution.py:51
  107.8 3.8 %convert_reduce_fusion = (f32[640]{0:T(1024)S(1)}, bf16[1,1,1024,640]{3,2,1,0:T(8,128)(2,1)S(1)}) fusion(bf16[1024,640]{1,0:T(8,128)(2,1)S(1)} %bitcast.89, bf16[9,640,640]{1,2,0:T(8,128)(2,1)} %all-gather.5.cloned.1.call-done, f32[1024,640]{1,0:T(8,128)S(1)} %fusion.39, f32[1024,640]{1,0:T(8,128)S(1)} %fusion.40, f32[1024,640]{1,0:T(8,128)S(1)} %fusion.41, ...), kind=kOutput, calls=%fused_computation.6 | convolution fusion | flops 847379840 | bytes 25725440 | tf_op jit(solution)/shard_map/dot_general | solution.py:51
  112.0 0.4 fusion.5
  112.9 2.1 %fusion.12 = bf16[1,1,1024,640]{3,2,1,0:T(8,128)(2,1)} fusion(bf16[1,1,1024,640]{3,2,1,0:T(8,128)(2,1)S(1)} %get-tuple-element.14, f32[640]{0:T(1024)S(1)} %copy-done.11, f32[640]{0:T(1024)S(1)} %mul.92, f32[640]{0:T(1024)S(1)} %sub.61), kind=kLoop, calls=%fused_computation.21 | loop fusion | flops 5898240 | bytes 2629120 | tf_op jit(solution)/shard_map/convert_element_type | solution.py:32
  115.0 3.3 %collective-permute-start = (bf16[1,1,1024,640]{3,2,1,0:T(8,128)(2,1)}, bf16[1,1,1024,640]{3,2,1,0:T(8,128)(2,1)}, u32[]{:S(2)}, u32[]{:S(2)}) collective-permute-start(bf16[1,1,1024,640]{3,2,1,0:T(8,128)(2,1)} %fusion.12), channel_id=1, source_target_pairs={{0,4},{4,8},{8,12},{12,16},{16,20},{20,24},{24,28},{1,5},{5,9},{9,... | collective-permute-start | bytes 3932168 | tf_op jit(solution)/shard_map/ppermute | solution.py:19
  118.3 1.3 collective-permute-start.1
  120.2 8.0 %all-gather = bf16[4,1,640]{2,1,0:T(2,128)(2,1)S(1)} all-gather(bf16[1,1,640]{2,1,0:T(2,128)(2,1)S(1)} %convert_bitcast_fusion), channel_id=1, replica_groups=mesh['fsdp'=8,'batch'=4] {'batch'}, dimensions={0}, use_global_device_ids=true | all-gather | bytes 6400 | tf_op jit(solution)/shard_map/all_gather | solution.py:84
  128.6 3.2 %fusion.31 = f32[1024,640]{1,0:T(8,128)S(1)} fusion(bf16[1,1,1024,640]{3,2,1,0:T(8,128)(2,1)} %fusion.12, bf16[3,640,640]{1,2,0:T(8,128)(2,1)} %all-gather.7.cloned.1.call-done), kind=kOutput, calls=%fused_computation.46 | convolution fusion | flops 838860800 | bytes 4751360 | tf_op jit(solution)/shard_map/dot_general | solution.py:59
  131.9 2.7 %fusion.33 = f32[1024,640]{1,0:T(8,128)S(1)} fusion(bf16[1,1,1024,640]{3,2,1,0:T(8,128)(2,1)} %collective-permute-done, bf16[3,640,640]{1,2,0:T(8,128)(2,1)S(1)} %copy-done.9), kind=kOutput, calls=%fused_computation.48 | convolution fusion | flops 838860800 | bytes 4751360 | tf_op jit(solution)/shard_map/dot_general | solution.py:59
  134.6 2.6 %fusion.22 = bf16[1,1,1024,640]{3,2,1,0:T(8,128)(2,1)} fusion(bf16[1,1,1024,640]{3,2,1,0:T(8,128)(2,1)S(1)} %get-tuple-element.14, f32[1024,640]{1,0:T(8,128)S(1)} %fusion.33, f32[1024,640]{1,0:T(8,128)S(1)} %fusion.31, bf16[1,1,1024,640]{3,2,1,0:T(8,128)(2,1)S(1)} %collective-permute-done.1, bf16[3,640,640]{1,2,0:T(8,128)(2,1)S(1)} %copy-done.9), kind=kOutput, calls=%fused_computation.31 | convolution fusion | flops 842137600 | bytes 9994240 | tf_op jit(solution)/shard_map/dot_general | solution.py:59
  137.1 1.7 reshape.208
  138.8 2.4 %convolution_convert_fusion = bf16[64,20480]{1,0:T(8,128)(2,1)} fusion(bf16[32,20480]{1,0:T(8,128)(2,1)S(1)} %reshape.208, s32[32]{0:T(128)S(1)} %multiply_add_fusion, pred[]{:T(512)} %bitcast.28), kind=kOutput, calls=%fused_computation | convolution fusion | flops 85200896 | bytes 3932289 | tf_op jit(solution)/shard_map/dot_general | solution.py:79
  141.2 4.5 %reshape_reshape.6 = bf16[4,512,640]{2,1,0:T(8,128)(2,1)} reshape(bf16[64,20480]{1,0:T(8,128)(2,1)} %convolution_convert_fusion) | data formatting | bytes 5242880 | tf_op jit(solution)/shard_map/reshape;reshape | solution.py:88
  145.7 19.9 %all-gather.9.cloned.1.call-done = bf16[4,640,640]{2,1,0:T(8,128)(2,1)} async-done(((bf16[1,640,640]{2,1,0:T(8,128)(2,1)}), bf16[4,640,640]{2,1,0:T(8,128)(2,1)}) %all-gather.9.cloned.1.call-update) | async-done | bytes 3276816 | tf_op jit(solution)/shard_map/all_gather | solution.py:83
  165.6 10.0 %fusion.26 = bf16[4,512,640]{2,1,0:T(8,128)(2,1)} fusion(bf16[4,640,640]{2,1,0:T(8,128)(2,1)} %all-gather.9.cloned.1.call-done, f32[4,640]{1,0:T(4,128)S(1)} %bitcast.97, bf16[4,512,640]{2,1,0:T(8,128)(2,1)} %reshape_reshape.6), kind=kOutput, calls=%fused_computation.35 | convolution fusion | flops 3361996800 | bytes 8529920 | tf_op jit(solution)/shard_map/gth,gch->gtc/dot_general | solution.py:91
  175.6 4.5 %reshape_reshape.7 = bf16[64,20480]{1,0:T(8,128)(2,1)} reshape(bf16[4,512,640]{2,1,0:T(8,128)(2,1)} %fusion.26) | data formatting | bytes 5242880 | tf_op jit(solution)/shard_map/reshape;reshape | solution.py:96
  180.1 2.3 %fusion = bf16[32,20480]{1,0:T(8,128)(2,1)S(1)} fusion(bf16[64,20480]{1,0:T(8,128)(2,1)} %reshape_reshape.7, bf16[32,20480]{1,0:T(8,128)(2,1)S(1)} %reshape.208, s32[32]{0:T(128)S(1)} %multiply_add_fusion, pred[]{:T(512)} %bitcast.28), kind=kOutput, calls=%fused_computation.2 | convolution fusion | flops 85856256 | bytes 5243009 | tf_op jit(solution)/shard_map/dot_general | solution.py:95
  182.4 1.5 reshape.210
  (61 shorter events, 2.3 us)
Async XLA Ops:
  6.5 2.2 %copy-start = (bf16[1,1,1024,640]{3,2,1,0:T(8,128)(2,1)S(1)}, bf16[1,1,1024,640]{3,2,1,0:T(8,128)(2,1)}, u32[]{:S(2)}) copy-start(bf16[1,1,1024,640]{3,2,1,0:T(8,128)(2,1)} %param.9) | copy-start | bytes 3932164
  6.5 3.7 %copy-start.10 = (f32[640]{0:T(1024)S(1)}, f32[640]{0:T(1024)}, u32[]{:S(2)}) copy-start(f32[640]{0:T(1024)} %param.10) | copy-start | bytes 7684
  6.5 78.8 %all-gather.5.cloned.1.call-start = ((), (), s32[]{:S(2)}) async-start(), calls=%async_computation | async-start | bytes 8294400 | tf_op jit(solution)/shard_map/all_gather | solution.py:44
  7.3 121.4 %all-gather.7.cloned.1.call-start = ((), (), s32[]{:S(2)}) async-start(), calls=%async_computation.1 | async-start | bytes 2764800 | tf_op jit(solution)/shard_map/all_gather | solution.py:56
  8.0 157.6 %all-gather.9.cloned.1.call-start = ((), (), s32[]{:S(2)}) async-start(), calls=%async_computation.2 | async-start | bytes 4096000 | tf_op jit(solution)/shard_map/all_gather | solution.py:83
  85.4 2.6 %copy-start.8 = (bf16[1,32,32,640]{3,2,1,0:T(8,128)(2,1)S(1)}, bf16[1,32,32,640]{3,2,1,0:T(8,128)(2,1)}, u32[]{:S(2)}) copy-start(bf16[1,32,32,640]{3,2,1,0:T(8,128)(2,1)} %get-tuple-element.11) | copy-start | bytes 3932164
  87.9 2.6 %copy-start.7 = (bf16[1,32,32,640]{3,2,1,0:T(8,128)(2,1)S(1)}, bf16[1,32,32,640]{3,2,1,0:T(8,128)(2,1)}, u32[]{:S(2)}) copy-start(bf16[1,32,32,640]{3,2,1,0:T(8,128)(2,1)} %get-tuple-element.10) | copy-start | bytes 3932164
  90.5 2.6 %copy-start.6 = (bf16[1,32,32,640]{3,2,1,0:T(8,128)(2,1)S(1)}, bf16[1,32,32,640]{3,2,1,0:T(8,128)(2,1)}, u32[]{:S(2)}) copy-start(bf16[1,32,32,640]{3,2,1,0:T(8,128)(2,1)} %get-tuple-element.9) | copy-start | bytes 3932164
  93.1 2.7 %copy-start.5 = (bf16[1,32,32,640]{3,2,1,0:T(8,128)(2,1)S(1)}, bf16[1,32,32,640]{3,2,1,0:T(8,128)(2,1)}, u32[]{:S(2)}) copy-start(bf16[1,32,32,640]{3,2,1,0:T(8,128)(2,1)} %get-tuple-element.8) | copy-start | bytes 3932164
  95.9 2.6 %copy-start.4 = (bf16[1,32,32,640]{3,2,1,0:T(8,128)(2,1)S(1)}, bf16[1,32,32,640]{3,2,1,0:T(8,128)(2,1)}, u32[]{:S(2)}) copy-start(bf16[1,32,32,640]{3,2,1,0:T(8,128)(2,1)} %get-tuple-element.7) | copy-start | bytes 3932164
  98.5 2.6 %copy-start.3 = (bf16[1,32,32,640]{3,2,1,0:T(8,128)(2,1)S(1)}, bf16[1,32,32,640]{3,2,1,0:T(8,128)(2,1)}, u32[]{:S(2)}) copy-start(bf16[1,32,32,640]{3,2,1,0:T(8,128)(2,1)} %get-tuple-element.6) | copy-start | bytes 3932164
  101.1 2.6 %copy-start.2 = (bf16[1,32,32,640]{3,2,1,0:T(8,128)(2,1)S(1)}, bf16[1,32,32,640]{3,2,1,0:T(8,128)(2,1)}, u32[]{:S(2)}) copy-start(bf16[1,32,32,640]{3,2,1,0:T(8,128)(2,1)} %get-tuple-element.12) | copy-start | bytes 3932164
  103.7 4.1 %copy-start.1 = (bf16[1,32,32,640]{3,2,1,0:T(8,128)(2,1)S(1)}, bf16[1,32,32,640]{3,2,1,0:T(8,128)(2,1)}, u32[]{:S(2)}) copy-start(bf16[1,32,32,640]{3,2,1,0:T(8,128)(2,1)} %get-tuple-element.5) | copy-start | bytes 3932164
  107.8 5.0 %copy-start.11 = (f32[640]{0:T(1024)S(1)}, f32[640]{0:T(1024)}, u32[]{:S(2)}) copy-start(f32[640]{0:T(1024)} %param.11) | copy-start | bytes 7684
  111.6 8.0 %copy-start.12 = (f32[1,640]{1,0:T(1,128)S(1)}, f32[1,640]{1,0:T(1,128)}, u32[]{:S(2)}) copy-start(f32[1,640]{1,0:T(1,128)} %param.15) | copy-start | bytes 7684
  111.6 16.7 %copy-start.13 = (s32[1,32,1]{1,2,0:T(1,128)S(1)}, s32[1,32,1]{1,2,0:T(1,128)}, u32[]{:S(2)}) copy-start(s32[1,32,1]{1,2,0:T(1,128)} %param.16) | copy-start | bytes 388
  115.0 16.9 %collective-permute-start = (bf16[1,1,1024,640]{3,2,1,0:T(8,128)(2,1)}, bf16[1,1,1024,640]{3,2,1,0:T(8,128)(2,1)}, u32[]{:S(2)}, u32[]{:S(2)}) collective-permute-start(bf16[1,1,1024,640]{3,2,1,0:T(8,128)(2,1)} %fusion.12), channel_id=1, source_target_pairs={{0,4},{4,8},{8,12},{12,16},{16,20},{20,24},{24,28},{1,5},{5,9},{9,... | collective-permute-start | bytes 3932168 | tf_op jit(solution)/shard_map/ppermute | solution.py:19
  118.3 16.3 %collective-permute-start.1 = (bf16[1,1,1024,640]{3,2,1,0:T(8,128)(2,1)}, bf16[1,1,1024,640]{3,2,1,0:T(8,128)(2,1)S(1)}, u32[]{:S(2)}, u32[]{:S(2)}) collective-permute-start(bf16[1,1,1024,640]{3,2,1,0:T(8,128)(2,1)} %fusion.12), channel_id=1, source_target_pairs={{4,0},{8,4},{12,8},{16,12},{20,16},{24,20},{28,24},{5,1},{9,5},{13... | collective-permute-start | bytes 3932168 | tf_op jit(solution)/shard_map/ppermute | solution.py:20
  128.6 3.3 %copy-start.9 = (bf16[3,640,640]{1,2,0:T(8,128)(2,1)S(1)}, bf16[3,640,640]{1,2,0:T(8,128)(2,1)}, u32[]{:S(2)}) copy-start(bf16[3,640,640]{1,2,0:T(8,128)(2,1)} %all-gather.7.cloned.1.call-done) | copy-start | bytes 7372804
Sparse Core Ops, SparseCore 0:
  9.0 76.3 all-gather.4
  87.0 31.0 all-gather.6
  119.9 45.6 all-gather.8
where the time goes:
time: 191 us; the launch traced here: 190 us
  waiting for transfers between devices  91 us (48%)
  matrix products  49.1 us (26%)
  local copies, waits for them, and re-layouts  18.6 us (10%)
  between operations  14.2 us (7%)
  blocking collectives  8.04 us (4%)
  other arithmetic  4.8 us (3%)
  starting transfers between devices  4.64 us (2%)
    all_gather x1, waiting for transfers between devices, per_device(): piece = lax.all_gather(spatial_w, 'fsdp', axis=2, tiled=True)  69 us
    dot_general x9, matrix products, per_device(): jnp.dot(window, piece[offset], preferred_element_type=jnp.float32)  26 us
    all_gather x1, waiting for transfers between devices, per_device(): weights = lax.all_gather(critic_w, 'batch', axis=0, tiled=True)  19.9 us
    dot_general x1, matrix products, per_device(): jnp.einsum('gth,gch->gtc', slope, weights, preferred_element_type=jnp.flo...  10 us
    dot_general x3, matrix products, per_device(): jnp.dot(beside_all[:, tap].reshape(-1, width), piece[tap], preferred_elem...  8.43 us
    all_gather x1, blocking collectives, per_device(): lax.all_gather(critic_head.astype(jnp.bfloat16), 'batch', axis=0, tiled=T...  8.04 us
    slice x1, local copies, waits for them, and re-layouts, per_device(): padded[:, row_off:row_off + IMG_ROWS, col_off:col_off + IMG_COLS]  5.3 us
    another operation x1, local copies, waits for them, and re-layouts, per_device(): block = outgoing.reshape(count, -1, width)  4.5 us
  transfers between devices with their start and end apart: 5, of which 2 were waited for; matrix products, arithmetic and copies ran while one was open for 28% of the time, Pallas kernels for 0%

commit v1 on v0

--- a/solution.py
+++ b/solution.py
@@ -1,12 +1,33 @@
+import functools
+
 import jax
 import jax.numpy as jnp
 from jax import lax
+from jax.experimental import pallas as pl
+from jax.experimental.pallas import tpu as pltpu
 from jax.sharding import PartitionSpec as P
 
 GROUPS = 32
 IMG_ROWS = 32
 IMG_COLS = 32
 PIX = 1024
+F32 = jnp.float32
+BF16 = jnp.bfloat16
+MESH = pl.DeviceIdType.MESH
+NT = (((1,), (1,)), ((), ()))
+
+
+def ring_gather(piece, axis, dim):
+    size, me = lax.axis_size(axis), lax.axis_index(axis)
+    length = piece.shape[dim]
+    shape = piece.shape[:dim] + (length * size,) + piece.shape[dim + 1 :]
+    whole = jnp.zeros(shape, piece.dtype)
+    whole = lax.dynamic_update_slice_in_dim(whole, piece, me * length, dim)
+    for step in range(1, size):
+        piece = lax.ppermute(piece, axis, [(i, (i + 1) % size) for i in range(size)])
+        owner = lax.rem(me - step + size, size)
+        whole = lax.dynamic_update_slice_in_dim(whole, piece, owner * length, dim)
+    return whole
 
 
 def with_halo(array, sides, width):
@@ -41,7 +62,7 @@
     padded = jnp.pad(
         first.reshape(cands, IMG_ROWS, IMG_COLS, width), ((0, 0), (1, 1), (1, 1), (0, 0))
     )
-    piece = lax.all_gather(spatial_w, "fsdp", axis=2, tiled=True)
+    piece = ring_gather(spatial_w, "fsdp", 2)
     total = jnp.zeros((cands * PIX, piece.shape[2]), jnp.float32)
     for offset in range(9):
         row_off, col_off = divmod(offset, 3)
@@ -53,7 +74,7 @@
     section = (latents.astype(jnp.float32) + mixed.reshape(latents.shape)).astype(jnp.bfloat16)
     second = group_silu(section, second_gain)
     beside_all = with_halo(second, (("fsdp", 1),), 1)
-    piece = lax.all_gather(temporal_w, "fsdp", axis=2, tiled=True)
+    piece = ring_gather(temporal_w, "fsdp", 2)
     total = jnp.zeros((cands * PIX, piece.shape[2]), jnp.float32)
     for tap in range(3):
         total = total + jnp.dot(
@@ -67,7 +88,9 @@
     chosen = (flat_targets[:, None] == jnp.arange(groups, dtype=jnp.int32)[None, :]).astype(
         jnp.int32
     )
-    earlier = jnp.cumsum(chosen, axis=0) - chosen
+    spot = jnp.arange(chosen.shape[0], dtype=jnp.int32)
+    before = (spot[None, :, None] < spot[:, None, None]).astype(jnp.int32)
+    earlier = jnp.sum(before * chosen[None], axis=1)
     slot_of = jnp.sum(earlier * chosen, axis=1)
     live = jnp.repeat(feasible.reshape(-1), IMG_ROWS) > 0
     position = flat_targets * slots + slot_of
@@ -80,10 +103,8 @@
         .astype(jnp.bfloat16)
         .reshape(groups, slots, IMG_COLS * width)
     )
-    weights = lax.all_gather(critic_w, "batch", axis=0, tiled=True)
-    heads = lax.all_gather(critic_head.astype(jnp.bfloat16), "batch", axis=0, tiled=True).astype(
-        jnp.float32
-    )
+    weights = ring_gather(critic_w, "batch", 0)
+    heads = ring_gather(critic_head, "batch", 0)
     count = weights.shape[0]
     block = outgoing.reshape(count, -1, width)
     pre = jnp.einsum("gtc,gch->gth", block, weights, preferred_element_type=jnp.float32)
@@ -97,6 +118,396 @@
     )
     guided = (rows.astype(jnp.float32) - back).astype(jnp.bfloat16)
     return guided.reshape(latents.shape)
+
+
+def moments(sums, spread_matrix):
+    wide = jnp.broadcast_to(sums, (8, sums.shape[1]))
+    return jnp.dot(
+        wide, spread_matrix, precision=lax.Precision.HIGHEST, preferred_element_type=F32
+    )[0:1]
+
+
+def fused_kernel(
+    latents, gain1, gain2, mine, critic_mine, heads_mine, same, targets, feasible,
+    out,
+    weights, critics, heads, shifted, mixed, section, frames, denoised,
+    up_send, down_send, z_recv, a_send, a_recv, b_send, b_recv, s_send, s_recv,
+    ca_send, ca_recv, cb_send, cb_recv, cs_send, cs_recv, h_send, h_recv,
+    f_send, f_recv, local_sem,
+):
+    C = latents.shape[1]
+    part = mine.shape[1]
+    fs, b = lax.axis_index("fsdp"), lax.axis_index("batch")
+    z, c = fs // 2, fs % 2
+    zs = 4
+    x_peer, y_peer = b + 1 - 2 * (b % 2), b + 2 - 4 * (b // 2)
+    peer_a = (1 - c) * x_peer + c * y_peer
+    peer_b = c * x_peer + (1 - c) * y_peer
+    peer_d = 3 - b
+    sib = (fs + 1 - 2 * c, b)
+    up, down = (fs + 2, b), (fs - 2, b)
+    to_a, to_b, to_d = (fs, peer_a), (fs, peer_b), (fs, peer_d)
+    far = (fs + 2 * c - 1, b)
+    has_up, has_down = z < zs - 1, z > 0
+    has_far = ((c == 1) & (z < zs - 1)) | ((c == 0) & (z > 0))
+
+    barrier = pltpu.get_barrier_semaphore()
+    for to in (sib, to_a, to_b, to_d):
+        pl.semaphore_signal(barrier, inc=1, device_id=to, device_id_type=MESH)
+
+    @pl.when(has_up)
+    def _():
+        pl.semaphore_signal(barrier, inc=1, device_id=up, device_id_type=MESH)
+
+    @pl.when(has_down)
+    def _():
+        pl.semaphore_signal(barrier, inc=1, device_id=down, device_id_type=MESH)
+
+    @pl.when(has_far)
+    def _():
+        pl.semaphore_signal(barrier, inc=1, device_id=far, device_id_type=MESH)
+
+    met = 4 + has_up.astype(jnp.int32) + has_down.astype(jnp.int32) + has_far.astype(jnp.int32)
+    pl.semaphore_wait(barrier, met)
+
+    def send(src, dst, ss, rs, to):
+        return pltpu.make_async_remote_copy(
+            src_ref=src, dst_ref=dst, send_sem=ss, recv_sem=rs, device_id=to, device_id_type=MESH
+        )
+
+    def slab(quarter, level, core, t):
+        rows = pl.ds(pl.multiple_of((2 * level + core) * part, 16), part)
+        return weights.at[quarter, rows, pl.ds(t * C, C)]
+
+    def shard(level, core, t):
+        rows = pl.ds(pl.multiple_of((2 * level + core) * part, 16), part)
+        return weights.at[:, rows, pl.ds(t * C, C)]
+
+    def own(quarter, t):
+        return mine.at[quarter, :, pl.ds(t * C, C)]
+
+    def z_copy(level, t, to, sems, first):
+        src = own(b, t) if first else slab(b, level, c, t)
+        return send(src, slab(b, level, c, t), sems.at[level, t], z_recv.at[level, t], to)
+
+    def a_copy(level, t):
+        return send(slab(b, level, c, t), slab(b, level, c, t), a_send.at[level, t], a_recv.at[level, t], to_a)
+
+    def b_copy(level, t, j):
+        q = b if j == 0 else peer_a
+        return send(slab(q, level, c, t), slab(q, level, c, t), b_send.at[level, t, j], b_recv.at[level, t, j], to_b)
+
+    def s_copy(level, t, first=False):
+        src = mine.at[:, :, pl.ds(t * C, C)] if first else shard(level, c, t)
+        return send(src, shard(level, c, t), s_send.at[level, t], s_recv.at[level, t], sib)
+
+    for t in range(3):
+
+        @pl.when(has_up)
+        def _():
+            z_copy(z, t, up, up_send, True).start()
+
+        @pl.when(has_down)
+        def _():
+            z_copy(z, t, down, down_send, True).start()
+
+        s_copy(z, t, True).start()
+    into = pltpu.make_async_copy(
+        mine, weights.at[:, pl.ds(pl.multiple_of(fs * part, 16), part), :], local_sem.at[0]
+    )
+    into.start()
+    own_critic = pltpu.make_async_copy(critic_mine, critics.at[b], local_sem.at[1])
+    own_critic.start()
+    own_head = pltpu.make_async_copy(heads_mine, heads.at[b], local_sem.at[2])
+    own_head.start()
+
+    def h_copy(j, to):
+        return send(heads_mine, heads.at[b], h_send.at[j], h_recv.at[j], to)
+
+    for j, to in enumerate((to_a, to_b, to_d)):
+        h_copy(j, to).start()
+
+    scale = 1.0 / (PIX * (C // GROUPS))
+
+    def stats(load):
+        def add(r, total):
+            v = load(r)
+            return total + jnp.sum(v, axis=0, keepdims=True)
+
+        center = moments(lax.fori_loop(0, IMG_ROWS, add, jnp.zeros((1, C), F32)), same[...]) * scale
+
+        def add_sq(r, total):
+            v = load(r) - center
+            return total + jnp.sum(v * v, axis=0, keepdims=True)
+
+        var = moments(lax.fori_loop(0, IMG_ROWS, add_sq, jnp.zeros((1, C), F32)), same[...]) * scale
+        return center, lax.rsqrt(var + 1e-05)
+
+    def at_row(r):
+        return pl.ds(pl.multiple_of(r * IMG_COLS, IMG_COLS), IMG_COLS)
+
+    def load_latent(r):
+        return latents[at_row(r), :].astype(F32)
+
+    center1, inv1 = stats(load_latent)
+    edge = jnp.zeros((IMG_COLS, 3 * C), BF16)
+    shifted[0:IMG_COLS, :] = edge
+    shifted[PIX + IMG_COLS : PIX + 2 * IMG_COLS, :] = edge
+    column = lax.broadcasted_iota(jnp.int32, (IMG_COLS, C), 0)
+
+    @pl.loop(0, IMG_ROWS)
+    def _(r):
+        v = (load_latent(r) - center1) * inv1 * gain1[...]
+        v = v / (1.0 + jnp.exp(-v))
+        where = pl.ds(pl.multiple_of((r + 1) * IMG_COLS, IMG_COLS), IMG_COLS)
+        shifted[where, 0:C] = jnp.where(column == 0, 0.0, pltpu.roll(v, 1, 0)).astype(BF16)
+        shifted[where, C : 2 * C] = v.astype(BF16)
+        shifted[where, 2 * C : 3 * C] = jnp.where(
+            column == IMG_COLS - 1, 0.0, pltpu.roll(v, IMG_COLS - 1, 0)
+        ).astype(BF16)
+
+    MB = 256
+    width = 2 * part
+
+    def conv(level):
+        rows = pl.ds(pl.multiple_of(level * width, 16), width)
+
+        @pl.loop(0, PIX // MB)
+        def _(m):
+            total = jnp.zeros((MB, width), F32)
+            for a in range(3):
+                x = shifted[pl.ds(pl.multiple_of(m * MB + a * IMG_COLS, IMG_COLS), MB), :]
+                total = total + lax.dot_general(x, weights[a, rows, :], NT, preferred_element_type=F32)
+            mixed[level, pl.ds(pl.multiple_of(m * MB, MB), MB), :] = total
+
+    k0 = jnp.where(z < 2, z + 1, z - 1)
+    k1 = jnp.where(z == 0, 2, jnp.where(z == 1, 0, jnp.where(z == 2, 3, 1)))
+    k2 = jnp.where(z < 2, 3, 0)
+    steps = [(k, t) for k in (k0, k1, k2) for t in range(3)]
+    half = C // 2
+
+    def crit(who):
+        return critics.at[who, pl.ds(pl.multiple_of(c * half, 16), half), :]
+
+    def ca_copy():
+        return send(critic_mine.at[pl.ds(pl.multiple_of(c * half, 16), half), :], crit(b), ca_send, ca_recv, to_a)
+
+    def cb_copy(j):
+        if j == 0:
+            src, who = critic_mine.at[pl.ds(pl.multiple_of(c * half, 16), half), :], b
+        else:
+            src, who = crit(peer_a), peer_a
+        return send(src, crit(who), cb_send.at[j], cb_recv.at[j], to_b)
+
+    def cs_copy(j):
+        who = (peer_a, peer_b, peer_d)[j]
+        return send(crit(who), crit(who), cs_send.at[j], cs_recv.at[j], sib)
+
+    into.wait()
+    for i in range(len(steps) + 2):
+        if i < len(steps):
+            k, t = steps[i]
+            z_copy(k, t, up, up_send, False).wait_recv()
+
+            @pl.when((k < z) & has_up)
+            def _():
+                z_copy(k, t, up, up_send, False).start()
+
+            @pl.when((k > z) & has_down)
+            def _():
+                z_copy(k, t, down, down_send, False).start()
+
+            a_copy(k, t).start()
+        if 1 <= i <= len(steps):
+            k, t = steps[i - 1]
+            a_copy(k, t).wait_recv()
+            for j in range(2):
+                b_copy(k, t, j).start()
+        if i >= 2:
+            k, t = steps[i - 2]
+            for j in range(2):
+                b_copy(k, t, j).wait_recv()
+            s_copy(k, t).start()
+        if i == 2:
+            for t in range(3):
+                s_copy(z, t).wait_recv()
+            conv(z)
+        if i == 6:
+            for t in range(3):
+                s_copy(k0, t).wait_recv()
+            conv(k0)
+        if i == 9:
+            ca_copy().start()
+            cb_copy(0).start()
+            for t in range(3):
+                s_copy(k1, t).wait_recv()
+            conv(k1)
+    for t in range(3):
+        s_copy(k2, t).wait_recv()
+    ca_copy().wait_recv()
+    cb_copy(1).start()
+    conv(k2)
+
+    @pl.loop(0, IMG_ROWS)
+    def _(r):
+        here = at_row(r)
+        whole = jnp.concatenate([mixed[l, here, :] for l in range(zs)], axis=1)
+        section[here, :] = (load_latent(r) + whole).astype(BF16)
+
+    def load_section(r):
+        return section[at_row(r), :].astype(F32)
+
+    center2, inv2 = stats(load_section)
+    parts = 4
+    block = PIX // parts
+
+    def f_copy(j, p, to):
+        slot = c if j == 0 else 1 - c
+        rows = pl.ds(p * block, block)
+        return send(frames.at[1, rows, :], frames.at[slot * 2, rows, :], f_send.at[j, p], f_recv.at[j, p], to)
+
+    @pl.when(jnp.logical_not(has_far))
+    def _():
+        @pl.loop(0, IMG_ROWS)
+        def _(r):
+            frames[2 * c, at_row(r), :] = jnp.zeros((IMG_COLS, C), BF16)
+
+    for p in range(parts):
+
+        @pl.loop(p * (IMG_ROWS // parts), (p + 1) * (IMG_ROWS // parts))
+        def _(r):
+            v = (load_section(r) - center2) * inv2 * gain2[...]
+            frames[1, at_row(r), :] = (v / (1.0 + jnp.exp(-v))).astype(BF16)
+
+        @pl.when(has_far)
+        def _():
+            f_copy(1, p, far).start()
+
+        f_copy(0, p, sib).start()
+
+    for j in range(2):
+        cb_copy(j).wait_recv()
+    for j in range(3):
+        cs_copy(j).start()
+
+    own_critic.wait()
+    own_head.wait()
+    for j, to in enumerate((to_a, to_b, to_d)):
+        h_copy(j, to).wait_recv()
+    for j in range(3):
+        cs_copy(j).wait_recv()
+    listed = feasible[0].astype(F32)
+    for p in range(parts):
+        f_copy(0, p, sib).wait_recv()
+
+        @pl.when(has_far)
+        def _():
+            f_copy(1, p, far).wait_recv()
+
+        rows = slice(p * block, (p + 1) * block)
+        total = lax.dot_general(frames[0, rows, :], weights[3, :, 0:C], NT, preferred_element_type=F32)
+        for j in (1, 2):
+            total = total + lax.dot_general(
+                frames[j, rows, :], weights[3, :, j * C : (j + 1) * C], NT, preferred_element_type=F32
+            )
+        denoised[rows, :] = (section[rows, :].astype(F32) + total).astype(BF16)
+
+        @pl.loop(p * (IMG_ROWS // parts), (p + 1) * (IMG_ROWS // parts))
+        def _(r):
+            here = at_row(r)
+            g = targets[r]
+            w = critics[g]
+            hd = heads[g]
+            d = denoised[here, :]
+            pre = jnp.tanh(jnp.dot(d, w, preferred_element_type=F32))
+            slope = ((1.0 - pre * pre) * hd[0:1, :]).astype(BF16)
+            grad = lax.dot_general(slope, w, NT, preferred_element_type=F32).astype(BF16)
+            out[here, :] = (d.astype(F32) - listed * grad.astype(F32)).astype(BF16)
+
+    for t in range(3):
+        for level in (z, k0, k1, k2):
+            first = level is z
+
+            @pl.when(has_up & (level <= z))
+            def _():
+                z_copy(level, t, up, up_send, first).wait_send()
+
+            @pl.when(has_down & (level >= z))
+            def _():
+                z_copy(level, t, down, down_send, first).wait_send()
+
+            s_copy(level, t, first).wait_send()
+            if not first:
+                a_copy(level, t).wait_send()
+                for j in range(2):
+                    b_copy(level, t, j).wait_send()
+    ca_copy().wait_send()
+    for j in range(2):
+        cb_copy(j).wait_send()
+    for j, to in enumerate((to_a, to_b, to_d)):
+        h_copy(j, to).wait_send()
+        cs_copy(j).wait_send()
+    for p in range(parts):
+        f_copy(0, p, sib).wait_send()
+
+        @pl.when(has_far)
+        def _():
+            f_copy(1, p, far).wait_send()
+
+
+def fused(
+    latents, norm_gain, second_gain, spatial_w, temporal_w, critic_w, critic_head, targets, feasible
+):
+    C = latents.shape[-1]
+    part = spatial_w.shape[-1]
+    mine = jnp.concatenate([spatial_w, temporal_w]).reshape(4, 3, C, part)
+    mine = mine.transpose(0, 3, 1, 2).reshape(4, part, 3 * C)
+    group = jnp.arange(C, dtype=jnp.int32) // (C // GROUPS)
+    same = (group[:, None] == group[None, :]).astype(F32)
+    vmem = pl.BlockSpec(memory_space=pltpu.VMEM)
+    smem = pl.BlockSpec(memory_space=pltpu.SMEM)
+    dma = pltpu.SemaphoreType.DMA
+    guided = pl.pallas_call(
+        fused_kernel,
+        out_shape=jax.ShapeDtypeStruct((PIX, C), BF16),
+        in_specs=[vmem] * 7 + [smem] * 2,
+        out_specs=vmem,
+        scratch_shapes=[
+            pltpu.VMEM((4, C, 3 * C), BF16),
+            pltpu.VMEM((4, C, C), BF16),
+            pltpu.VMEM((4, 8, C), F32),
+            pltpu.VMEM((PIX + 2 * IMG_COLS, 3 * C), BF16),
+            pltpu.VMEM((4, PIX, 2 * part), F32),
+            pltpu.VMEM((PIX, C), BF16),
+            pltpu.VMEM((3, PIX, C), BF16),
+            pltpu.VMEM((PIX, C), BF16),
+            dma((4, 3)), dma((4, 3)), dma((4, 3)),
+            dma((4, 3)), dma((4, 3)),
+            dma((4, 3, 2)), dma((4, 3, 2)),
+            dma((4, 3)), dma((4, 3)),
+            dma, dma, dma((2,)), dma((2,)), dma((3,)), dma((3,)), dma((3,)), dma((3,)),
+            dma((2, parts_of_frame())), dma((2, parts_of_frame())), dma((3,)),
+        ],
+        compiler_params=pltpu.CompilerParams(
+            collective_id=0, has_side_effects=True, vmem_limit_bytes=58 * 2**20
+        ),
+        name="guided_block",
+    )(
+        latents.reshape(PIX, C),
+        norm_gain.reshape(1, C),
+        second_gain.reshape(1, C),
+        mine,
+        critic_w.reshape(C, C),
+        jnp.broadcast_to(critic_head, (8, C)),
+        same,
+        targets.reshape(-1),
+        feasible.reshape(-1),
+    )
+    return guided.reshape(latents.shape)
+
+
+def parts_of_frame():
+    return 4
 
 
 def solution(mesh):
@@ -111,7 +522,8 @@
         P("batch", None, None),
         P("batch", "fsdp"),
     )
+    body = fused if dict(mesh.shape) == {"fsdp": 8, "batch": 4} else per_device
     out_specs = P("batch", "fsdp", None, None)
     return jax.shard_map(
-        per_device, mesh=mesh, in_specs=in_specs, out_specs=out_specs, check_vma=False
-    )
+        body, mesh=mesh, in_specs=in_specs, out_specs=out_specs, check_vma=False
+    )

time: 191 us -> 117 us (0.61)
  Pallas kernels: 0 us -> 104 us
  waiting for transfers between devices: 91 us -> 0 us
  matrix products: 49.1 us -> 0 us
  between operations: 14.2 us -> 0.68 us
  local copies, waits for them, and re-layouts: 18.6 us -> 8.53 us
  blocking collectives: 8.04 us -> 0 us
  starting transfers between devices: 4.64 us -> 0 us
    pallas_call x0 -> x1, Pallas kernels: none -> 104 us  [fused(): pl.pallas_call(fused_kernel, out_shape=jax.ShapeDtypeStruct((PIX, C), BF1...]
    all_gather x3 -> x0, waiting for transfers between devices: 88.9 us -> none  [the longest x1 69 us: per_device(): piece = lax.all_gather(spatial_w, 'fsdp', axis=2, tiled=True)]
    dot_general x15 -> x0, matrix products: 49.1 us -> none  [the longest x9 26 us: per_device(): jnp.dot(window, piece[offset], preferred_element_type=jnp.float32)]
    another operation x2 -> x0, local copies, waits for them, and re-layouts: 9 us -> none  [the longest x1 4.5 us: per_device(): block = outgoing.reshape(count, -1, width)]
    all_gather x1 -> x0, blocking collectives: 8.04 us -> none  [per_device(): lax.all_gather(critic_head.astype(jnp.bfloat16), 'batch', axis=0, tiled=T...]
    slice x1 -> x0, local copies, waits for them, and re-layouts: 5.3 us -> none  [per_device(): padded[:, row_off:row_off + IMG_ROWS, col_off:col_off + IMG_COLS]]
    ppermute x2 -> x0, starting transfers between devices: 4.56 us -> none  [the longest x1 3.28 us: with_halo(): before = lax.ppermute(last, axis, up)]
    unnamed x29 -> x1, local copies, waits for them, and re-layouts: 0.07 us -> 2.49 us
  transfers between devices with their start and end apart: 5 -> 0, of which waited for: 2 -> 0; matrix products, arithmetic and copies ran while one was open for 28% -> 0% of each run, Pallas kernels for 0% -> 0%
where the time goes in v1:
time: 117 us; the launch traced here: 116 us
  Pallas kernels  104 us (89%)
  local copies, waits for them, and re-layouts  8.53 us (7%)
  other arithmetic  3.48 us (3%)
    pallas_call x1, Pallas kernels, fused(): pl.pallas_call(fused_kernel, out_shape=jax.ShapeDtypeStruct((PIX, C), BF1...  104 us
    unnamed x1, local copies, waits for them, and re-layouts  2.49 us

profile of v1, /device:TPU:0, one launch (start us, length us, event | category | flops | bytes accessed | tf_op | source)
XLA Modules:
  0.0 116.4 jit_solution(14598129004213119802)
XLA Ops:
  0.7 1.3 %reshape.54.gain1 = f32[1,640]{1,0:T(1,128)} reshape(f32[640]{0:T(1024)} %param.10) | data formatting | bytes 5120 | tf_op jit(solution)/shard_map/reshape | solution.py:497
  1.9 1.3 %reshape.55.gain2 = f32[1,640]{1,0:T(1,128)} reshape(f32[640]{0:T(1024)} %param.11) | data formatting | bytes 5120 | tf_op jit(solution)/shard_map/reshape | solution.py:498
  3.2 0.7 reduce
  3.9 0.6 broadcast_in_dim.10.heads_mine
  4.5 1.4 %pad_maximum_fusion = bf16[12,640,80]{1,2,0:T(8,128)(2,1)S(1)} fusion(bf16[3,640,80]{1,2,0:T(8,128)(2,1)} %param.13, bf16[9,640,80]{1,2,0:T(8,128)(2,1)} %param.12), kind=kLoop, calls=%fused_computation.2 | loop fusion | flops 614400 | bytes 2457600 | tf_op jit(solution)/shard_map/concatenate | solution.py:463
  5.9 0.6 copy.13
  6.6 2.3 %reshape.57.mine = bf16[4,80,1920]{2,1,0:T(8,128)(2,1)} reshape(bf16[4,80,3,640]{3,2,1,0:T(4,128)(2,1)S(1)} %bitcast.10) | data formatting | bytes 2457600 | tf_op jit(solution)/shard_map/reshape | solution.py:464
  8.8 1.4 %compare_convert_fusion.same = f32[640,640]{1,0:T(8,128)} fusion(s32[640]{0:T(1024)S(1)} %add_select_fusion), kind=kLoop, calls=%fused_computation.1 | loop fusion | flops 819200 | bytes 1640960 | tf_op jit(solution)/shard_map/convert_element_type | solution.py:466
  10.2 103.7 %guided_block.1 = bf16[1024,640]{1,0:T(8,128)(2,1)} custom-call(bf16[1024,640]{1,0:T(8,128)(2,1)} %bitcast.13, f32[1,640]{1,0:T(1,128)} %reshape.54.gain1, f32[1,640]{1,0:T(1,128)} %reshape.55.gain2, bf16[4,80,1920]{2,1,0:T(8,128)(2,1)} %reshape.57.mine, bf16[640,640]{1,0:T(8,128)(2,1)} %bitcast.14, f32[8,640]{1,0:T(8,128)} %broadcast_in_dim.10.heads_mine, ...), custom_call_target="tpu_custom_call" | custom-call | tf_op jit(solution)/shard_map/guided_block/pallas_call | solution.py:470
  113.9 2.5 %copy.16 = bf16[1,1,1024,640]{3,2,1,0:T(8,128)(2,1)} copy(bf16[1,1,1024,640]{3,2,1,0:T(8,128)(2,1)} %bitcast.11) | data formatting | bytes 2621440
  (1 shorter events, 0.0 us)
